TPU v7x, 32 devices: a whole 2x2x4 slice. The times are simulated.
32 devices in a mesh: dp: 8 (over y, x, core), tensor: 4 (over z).
Axes of the slice: x: 2, y: 2, z: 4, core: 2. Of those that a mesh axis runs over, the one named last changes fastest.
Arguments:
- hidden: bfloat16 [2048, 5120], P('dp', 'tensor'), may hold values from -6 to 6
- norm_gain: float32 [5120], replicated, may hold values from 0.1 to 1.9
- w_query: bfloat16 [5120, 8192], P(None, 'tensor'), may hold values from -0.078125 to 0.078125
- key_projection_weight: bfloat16 [5120, 1024], P(None, 'tensor'), may hold values from -0.078125 to 0.078125
- value_projection_weight: bfloat16 [5120, 1024], P(None, 'tensor'), may hold values from -0.078125 to 0.078125
- query_gain: float32 [128], replicated, may hold values from 1 to 4
- key_gain: float32 [128], replicated, may hold values from 0.5 to 2
- kv_pool: bfloat16 [3072, 8, 2, 16, 128], P(('dp', 'tensor')), may hold values from -102 to 102
- page_owner: int32 [8, 256], replicated, may hold values from 0 to 31, as said below
- page_slot: int32 [8, 256], replicated, may hold values from 0 to 95, as said below
- prefix_len: int32 [8], P('dp'), may hold values from 512 to 4096, as said below
- new_owner: int32 [8, 16, 1], P('dp'), may hold values from 0 to 7; in each aligned block of 16 rows (0 to 15, 16 to 31, ..., all dimensions but the last counted through in order) at most 2 rows name the same one
Outputs:
- attn_out: bfloat16 [2048, 8192], P('dp', 'tensor')
- fresh_page_store: bfloat16 [128, 8, 2, 16, 128], P('dp', 'tensor')
Inputs may be any that keep to these rules, and one draw needn't show every extreme that they name: `page_owner`: for each request, no device owns more than 12 of its pages, and some device owns exactly 12. `page_slot`: the pages that one device owns sit in distinct slots. `prefix_len`: one request has the most cached tokens and one the least. `new_owner`: no dp index stores more than 2 new pages of one request.
All inputs are finite; a program needn't handle non-finite values.
Results may differ from a plain program's by a relative error of at most 0.006.
The roundings to bfloat16 on the way count: a program that leaves them out, or rounds other values in their place, can miss the bound.
Values may be sent and summed in bfloat16 or wider, within the bound.
A program may use at most 128 MiB of HBM per device.

v0:
```python
import functools
import math

import jax
import jax.numpy as jnp
from jax import lax
from jax.experimental import pallas as pl
from jax.experimental.pallas import tpu as pltpu
from jax.sharding import PartitionSpec as P

HEAD_SIZE = 128
PAGE_TOKENS = 16
SPAN = 256
NCAP = 2
MOST_PAGES = 256


EPS = 1e-06
THETA = 1000000.0
NEG = -1e30


def rms_rows(values, gain):
    mean_square = jnp.mean(values * values, axis=-1, keepdims=True)
    return values * lax.rsqrt(mean_square + EPS) * gain


def rotate(values, positions):
    half_width = values.shape[-1] // 2
    exponent = jnp.arange(half_width, dtype=jnp.float32) * (-2.0 / values.shape[-1])
    freqs = jnp.power(jnp.float32(THETA), exponent)
    angles = positions.astype(jnp.float32)[:, None] * freqs[None, :]
    cosine = jnp.cos(angles)[:, None, :]
    sine = jnp.sin(angles)[:, None, :]
    first_half = values[..., :half_width]
    second_half = values[..., half_width:]
    return jnp.concatenate(
        [first_half * cosine - second_half * sine, second_half * cosine + first_half * sine],
        axis=-1,
    )


def collect(matches, payload, capacity):
    ranks = jnp.cumsum(matches.astype(jnp.int32), axis=1) - 1
    places = jnp.arange(capacity, dtype=jnp.int32)
    landed = matches[:, :, None] & (ranks[:, :, None] == places[None, None, :])
    picked = jnp.sum(jnp.where(landed, payload[:, :, None], 0), axis=1)
    return (picked, jnp.any(landed, axis=1))


def gather_kernel(key_heads, groups, capacity, early, picked_ref, pool_ref, first_ref, second_ref):
    row = pl.program_id(0)
    last = key_heads - 1

    def pick(c, target, at):
        slot = picked_ref[row * capacity + c]
        for t in range(groups):
            target[0, t, at] = pool_ref[slot, t * key_heads + last]

    def whole(c, carry):
        slot = picked_ref[row * capacity + c]
        for h in range(last):
            for t in range(groups):
                first_ref[0, t, h * capacity + c] = pool_ref[slot, t * key_heads + h]
        return carry

    lax.fori_loop(0, capacity, whole, 0)
    for c in range(early):
        pick(c, first_ref, last * capacity + c)
    for c in range(early, capacity):
        pick(c, second_ref, c - early)


def gather_pages(picked, pool, key_heads, early):
    rows, capacity = picked.shape
    groups = pool.shape[1] // key_heads
    page = pool.shape[2:]
    units = ((key_heads - 1) * capacity + early, capacity - early)
    block = lambda n: pl.BlockSpec((1, groups, n) + page, lambda r: (r, 0, 0, 0, 0, 0))
    return pl.pallas_call(
        functools.partial(gather_kernel, key_heads, groups, capacity, early),
        grid=(rows,),
        out_shape=[jax.ShapeDtypeStruct((rows, groups, n) + page, pool.dtype) for n in units],
        in_specs=[
            pl.BlockSpec(memory_space=pltpu.SMEM),
            pl.BlockSpec(memory_space=pltpu.VMEM),
        ],
        out_specs=[block(n) for n in units],
        compiler_params=pltpu.CompilerParams(vmem_limit_bytes=32 * 2**20),
        cost_estimate=pl.CostEstimate(flops=0, bytes_accessed=4 * pool.size, transcendentals=0),
        name="gather_pages",
    )(picked.reshape(-1), pool)


BLOCK_PAGES = 64
ROW_TILES = 8


def attention_kernel(
    group, scale, base, begins, ends, places_ref, length_ref, q_ref, k_ref, v_ref, pages_ref, *refs
):
    if ends:
        out_ref, keys, values, acc, top = refs[-5:]
    else:
        acc, top, keys, values = refs[-4:]
    length = length_ref[0]
    columns = BLOCK_PAGES * PAGE_TOKENS
    live_pages = (length + PAGE_TOKENS - 1) // PAGE_TOKENS
    full = length // columns
    blocks = (length + columns - 1) // columns
    ones = jnp.ones((PAGE_TOKENS, HEAD_SIZE), jnp.bfloat16)
    factor = scale * math.log2(math.e)

    def place(i, carry):
        for u in range(8):
            j = i * 8 + u
            source = places_ref[0, j]
            at = base + places_ref[1, j]
            keys[j] = pages_ref[source, at, 0]
            values[j, :, :HEAD_SIZE] = pages_ref[source, at, 1]
            values[j, :, HEAD_SIZE:] = ones
        return carry

    lax.fori_loop(0, (live_pages + 7) // 8, place, 0)

    def spare(j, carry):
        values[j] = jnp.zeros(values.shape[1:], jnp.bfloat16)
        keys[j] = jnp.zeros(keys.shape[1:], jnp.bfloat16)
        return carry

    lax.fori_loop((live_pages + 7) // 8 * 8, blocks * BLOCK_PAGES, spare, 0)
    rows = q_ref.shape[0]
    row_ids = lax.broadcasted_iota(jnp.int32, (rows, rows), 0)
    column_ids = lax.broadcasted_iota(jnp.int32, (rows, rows), 1)
    causal = row_ids >= column_ids
    span_keys = k_ref[...]
    span_values = jnp.concatenate(
        [v_ref[...], jnp.ones((rows, HEAD_SIZE), jnp.bfloat16)], axis=1
    )
    contract_last = (((1,), (1,)), ((), ()))

    def scores_of(query, key_rows):
        return (
            lax.dot_general(query, key_rows, contract_last, preferred_element_type=jnp.float32)
            * factor
        )

    if not begins:
        acc[...] = refs[0][...]
        top[...] = refs[1][...]

    for g in range(0, group, ROW_TILES):
        queries = [q_ref[:, (g + t) * HEAD_SIZE : (g + t + 1) * HEAD_SIZE] for t in range(ROW_TILES)]
        for t in range(ROW_TILES if begins else 0):
            recent = jnp.where(causal, scores_of(queries[t], span_keys), NEG)
            peak = jnp.max(recent, axis=1, keepdims=True)
            weights = jnp.exp2(recent - peak).astype(jnp.bfloat16)
            top[g + t] = jnp.broadcast_to(peak, (rows, HEAD_SIZE))
            acc[g + t] = jnp.dot(weights, span_values, preferred_element_type=jnp.float32)

        def step(i, masked):
            start = pl.multiple_of(i * BLOCK_PAGES, BLOCK_PAGES)
            key_rows = keys[pl.ds(start, BLOCK_PAGES)].reshape(columns, HEAD_SIZE)
            value_rows = values[pl.ds(start, BLOCK_PAGES)].reshape(columns, 2 * HEAD_SIZE)
            for t in range(ROW_TILES):
                scores = scores_of(queries[t], key_rows)
                if masked:
                    positions = i * columns + lax.broadcasted_iota(jnp.int32, scores.shape, 1)
                    scores = jnp.where(positions < length, scores, NEG)
                before = top[g + t][:, :1]
                peak = jnp.maximum(before, jnp.max(scores, axis=1, keepdims=True))
                weights = jnp.exp2(scores - peak).astype(jnp.bfloat16)
                acc[g + t] = acc[g + t] * jnp.exp2(before - peak) + jnp.dot(
                    weights, value_rows, preferred_element_type=jnp.float32
                )
                top[g + t] = jnp.broadcast_to(peak, (rows, HEAD_SIZE))

        lax.fori_loop(0, full, lambda i, c: (step(i, False), c)[1], 0)

        @pl.when(full < blocks)
        def _():
            step(full, True)

        for t in range(ROW_TILES if ends else 0):
            mixed = acc[g + t]
            out_ref[:, (g + t) * HEAD_SIZE : (g + t + 1) * HEAD_SIZE] = (
                mixed[:, :HEAD_SIZE] / mixed[:, HEAD_SIZE:]
            ).astype(jnp.bfloat16)


def attend(
    places, length, queries, new_keys, new_values, pages, h, key_heads, scale, base, state, out, ends
):
    rows, width = queries.shape
    part = width // key_heads
    group = part // HEAD_SIZE
    most = places.shape[1]
    in_specs = [
        pl.BlockSpec(memory_space=pltpu.SMEM),
        pl.BlockSpec(memory_space=pltpu.SMEM),
        pl.BlockSpec((rows, part), lambda i: (0, h)),
        pl.BlockSpec((rows, HEAD_SIZE), lambda i: (0, h)),
        pl.BlockSpec((rows, HEAD_SIZE), lambda i: (0, h)),
        pl.BlockSpec(pages.shape, lambda i: (0,) * pages.ndim),
    ]
    operands = [places, length, queries, new_keys, new_values, pages]
    state_shapes = [(group, rows, 2 * HEAD_SIZE), (group, rows, HEAD_SIZE)]
    state_specs = [pl.BlockSpec(shape, lambda i: (0, 0, 0)) for shape in state_shapes]
    if state is not None:
        in_specs += state_specs
        operands += state
    aliases = {}
    if ends and out is not None:
        in_specs.append(pl.BlockSpec(memory_space=pl.ANY))
        operands.append(out)
        aliases = {len(operands) - 1: 0}
    scratch = [
        pltpu.VMEM((most, PAGE_TOKENS, HEAD_SIZE), jnp.bfloat16),
        pltpu.VMEM((most, PAGE_TOKENS, 2 * HEAD_SIZE), jnp.bfloat16),
    ]
    if ends:
        out_shape = jax.ShapeDtypeStruct((rows, width), jnp.bfloat16)
        out_specs = pl.BlockSpec((rows, part), lambda i: (0, h))
        scratch += [pltpu.VMEM(shape, jnp.float32) for shape in state_shapes]
    else:
        out_shape = [jax.ShapeDtypeStruct(shape, jnp.float32) for shape in state_shapes]
        out_specs = state_specs
    return pl.pallas_call(
        functools.partial(attention_kernel, group, scale, base, state is None, ends),
        grid=(1,),
        out_shape=out_shape,
        in_specs=in_specs,
        out_specs=out_specs,
        scratch_shapes=scratch,
        input_output_aliases=aliases,
        compiler_params=pltpu.CompilerParams(vmem_limit_bytes=44 * 2**20),
        cost_estimate=pl.CostEstimate(
            flops=4 * rows * part * most * PAGE_TOKENS,
            bytes_accessed=2 * pages.size,
            transcendentals=rows * group * most * PAGE_TOKENS,
        ),
        name="attend_head",
    )(*operands)


def shards(
    hidden,
    norm_gain,
    w_query,
    key_projection_weight,
    value_projection_weight,
    query_gain,
    key_gain,
    kv_pool,
    page_owner,
    page_slot,
    prefix_len,
    new_owner,
):
    data_ways = lax.axis_size("dp")
    tensor_ways = lax.axis_size("tensor")
    request = lax.axis_index("dp")
    slot_count = kv_pool.shape[0]
    capacity = slot_count // data_ways
    key_heads = key_projection_weight.shape[1] // HEAD_SIZE
    local_heads = w_query.shape[1] // HEAD_SIZE
    scale = 1.0 / math.sqrt(HEAD_SIZE)
    own_row = lax.dynamic_index_in_dim(page_owner, request, 0, keepdims=False)
    my_device = request * tensor_ways + lax.axis_index("tensor")
    picked, unused = collect(page_owner == my_device, page_slot, capacity)
    early = max(1, capacity // 2)
    outgoing = gather_pages(picked, kv_pool, key_heads, early)
    sources = data_ways * tensor_ways

    def exchange(pages):
        return lax.all_to_all(
            pages.reshape((sources,) + pages.shape[2:]),
            ("dp", "tensor"),
            split_axis=0,
            concat_axis=0,
            tiled=True,
        )

    first_pages = exchange(outgoing[0])
    full_rows = lax.all_gather(hidden, "tensor", axis=1, tiled=True)
    full_rows, outgoing = lax.optimization_barrier((full_rows, outgoing))
    normalized_rows = rms_rows(full_rows.astype(jnp.float32), norm_gain).astype(jnp.bfloat16)
    length = prefix_len[0]
    offsets = jnp.arange(SPAN, dtype=jnp.int32)
    positions = length + offsets
    query_flat = jnp.dot(normalized_rows, w_query, preferred_element_type=jnp.float32).reshape(
        SPAN, local_heads, HEAD_SIZE
    )
    flattened_keys = jnp.dot(
        normalized_rows, key_projection_weight, preferred_element_type=jnp.float32
    ).reshape(SPAN, key_heads, HEAD_SIZE)
    queries = rotate(rms_rows(query_flat, query_gain), positions).astype(jnp.bfloat16)
    queries, first_pages, late = lax.optimization_barrier((queries, first_pages, outgoing[1]))
    second_pages = exchange(late)
    new_keys = rotate(rms_rows(flattened_keys, key_gain), positions).astype(jnp.bfloat16)
    fresh_value_rows = (
        jnp.dot(normalized_rows, value_projection_weight, preferred_element_type=jnp.float32)
        .astype(jnp.bfloat16)
        .reshape(SPAN, key_heads, HEAD_SIZE)
    )
    page_count = SPAN // PAGE_TOKENS
    stacked_pages = jnp.stack([new_keys, fresh_value_rows], axis=2)
    fresh_pages = (
        stacked_pages.reshape(page_count, PAGE_TOKENS, key_heads, 2, HEAD_SIZE)
        .transpose(0, 2, 3, 1, 4)
        .reshape(page_count, key_heads * 2 * PAGE_TOKENS * HEAD_SIZE)
    )
    targets = new_owner[0, :, 0]
    page_index = jnp.arange(page_count, dtype=jnp.int32)
    earlier = page_index[None, :] < page_index[:, None]
    ranks = jnp.sum((targets[:, None] == targets[None, :]) & earlier, axis=1)
    slot_index = jnp.arange(data_ways * NCAP, dtype=jnp.int32)
    selector = ((targets * NCAP + ranks)[None, :] == slot_index[:, None]).astype(jnp.bfloat16)
    outgoing_pages = jnp.dot(selector, fresh_pages, preferred_element_type=jnp.float32).astype(
        jnp.bfloat16
    )
    outgoing_pages = outgoing_pages.reshape(data_ways * NCAP, key_heads, 2, PAGE_TOKENS, HEAD_SIZE)
    outgoing_pages = outgoing_pages.reshape(
        (data_ways, NCAP) + outgoing_pages.shape[1:]
    )
    every = lax.all_gather(outgoing_pages, "dp", axis=0)
    same = own_row[:, None] == own_row[None, :]
    later = jnp.arange(MOST_PAGES)[:, None] > jnp.arange(MOST_PAGES)[None, :]
    page_ranks = jnp.sum(same & later, axis=1).astype(jnp.int32)
    live_tokens = jnp.clip(
        length - jnp.arange(MOST_PAGES, dtype=jnp.int32) * PAGE_TOKENS, 0, PAGE_TOKENS
    )
    everywhere = jnp.stack([own_row, page_ranks])

    def subset(chosen, shift):
        order = jnp.cumsum(chosen.astype(jnp.int32)) - 1
        landed = chosen[:, None] & (order[:, None] == jnp.arange(MOST_PAGES)[None, :])
        table = jnp.stack([own_row, page_ranks - shift])
        table = jnp.sum(jnp.where(landed[None], table[:, :, None], 0), axis=1)
        return (table, jnp.sum(jnp.where(chosen, live_tokens, 0)).reshape(1))

    first_table, first_length = subset(page_ranks < early, 0)
    second_table, second_length = subset(page_ranks >= early, early)
    tensors = (
        queries.reshape(SPAN, local_heads * HEAD_SIZE),
        new_keys.reshape(SPAN, key_heads * HEAD_SIZE),
        fresh_value_rows.reshape(SPAN, key_heads * HEAD_SIZE),
    )
    attn_out = None
    last = key_heads - 1
    for h in range(last):
        attn_out = attend(
            everywhere, prefix_len, *tensors, first_pages, h, key_heads, scale, h * capacity, None, attn_out, True
        )
    state = attend(
        first_table, first_length, *tensors, first_pages, last, key_heads, scale, last * capacity, None, None, False
    )
    every, state = lax.optimization_barrier((every, state))
    fresh_page_store = lax.dynamic_index_in_dim(every, request, 1, keepdims=False)
    fresh_page_store = fresh_page_store.reshape((data_ways * NCAP,) + outgoing_pages.shape[2:])
    attn_out = attend(
        second_table, second_length, *tensors, second_pages, last, key_heads, scale, 0, list(state), attn_out, True
    )
    return (attn_out, fresh_page_store)


def solution(mesh):
    return jax.shard_map(
        shards,
        mesh=mesh,
        in_specs=(
            P("dp", "tensor"),
            P(),
            P(None, "tensor"),
            P(None, "tensor"),
            P(None, "tensor"),
            P(),
            P(),
            P(("dp", "tensor"), None, None, None, None),
            P(),
            P(),
            P("dp"),
            P("dp", None, None),
        ),
        out_specs=(P("dp", "tensor"), P("dp", "tensor", None, None, None)),
        check_vma=False,
    )
```

profile of v0, /device:TPU:7, one launch (start us, length us, event | category | flops | bytes accessed | tf_op | source)
XLA Modules:
  0.0 233.0 jit_solution(5650121185540037970)
XLA Ops:
  7.2 0.7 all-gather.3.cloned.1.call-update
  7.9 0.7 convert_bitcast_fusion
  8.7 0.6 reduce-window.26
  9.2 0.2 slice_reduce_fusion
  9.5 0.1 add_bitcast_fusion
  9.6 1.0 select_reduce_fusion.2
  10.5 0.1 copy.37
  10.6 0.1 reshape.341.picked_ref
  10.7 2.8 %copy-done.2 = bf16[96,8,2,16,128]{4,3,2,1,0:T(8,128)(2,1)S(1)} copy-done((bf16[96,8,2,16,128]{4,3,2,1,0:T(8,128)(2,1)S(1)}, bf16[96,8,2,16,128]{4,3,2,1,0:T(8,128)(2,1)}, u32[]{:S(2)}) %copy-start.2) | copy-done | bytes 6291480
  13.5 4.0 %gather_pages.1 = (bf16[8,4,18,2,16,128]{5,4,3,2,1,0:T(8,128)(2,1)S(1)}, bf16[8,4,6,2,16,128]{5,4,3,2,1,0:T(8,128)(2,1)}) custom-call(s32[96]{0:T(128)S(1)} %reshape.341.picked_ref, bf16[96,8,2,16,128]{4,3,2,1,0:T(8,128)(2,1)S(1)} %copy-done.2), custom_call_target="tpu_custom_call" | custom-call | bytes 12582912 | tf_op jit(solution)/shard_map/gather_pages/pallas_call | solution.py:80
  17.5 2.2 copy-done.3
  19.6 6.4 %all-to-all-start = ((bf16[32,18,2,16,128]{4,3,2,1,0:T(8,128)(2,1)}), bf16[32,18,2,16,128]{4,3,2,1,0:T(8,128)(2,1)}, u32[]{:S(2)}, u32[]{:S(2)}) async-start(bf16[32,18,2,16,128]{4,3,2,1,0:T(8,128)(2,1)} %bitcast.54), calls=%async_computation | async-start | bytes 9437184 | tf_op jit(solution)/shard_map/all_to_all | solution.py:276
  26.1 0.0 all-gather.5.cloned.1.call-start
  26.8 0.7 constant_dynamic-slice_fusion.1
  27.5 0.2 convert_reduce_fusion.1
  27.7 0.2 convert_reduce_fusion
  27.9 0.7 select_reduce_fusion.3
  28.6 0.5 multiply_cosine_fusion
  29.1 88.5 %all-gather.3.cloned.1.call-done = bf16[256,5120]{1,0:T(8,128)(2,1)} async-done(((bf16[256,1280]{1,0:T(8,128)(2,1)}), bf16[256,5120]{1,0:T(8,128)(2,1)}) %all-gather.3.cloned.1.call-update) | async-done | bytes 2621456 | tf_op jit(solution)/shard_map/all_gather | solution.py:285
  117.6 2.5 %fusion = f32[256]{0:T(256)S(1)} fusion(bf16[256,5120]{1,0:T(8,128)(2,1)} %all-gather.3.cloned.1.call-done), kind=kLoop, calls=%fused_computation.3 | loop fusion | flops 3931904 | bytes 2622464 | tf_op jit(solution)/shard_map/reduce_sum | solution.py:24
  120.2 2.7 %convolution_convert_fusion.1.v_ref = bf16[256,256]{1,0:T(8,128)(2,1)S(1)} fusion(bf16[5120,256]{1,0:T(8,128)(2,1)} %param.16, bf16[256,5120]{1,0:T(8,128)(2,1)S(1)} %copy-done.13, f32[5120]{0:T(1024)S(1)} %copy-done.17, f32[256]{0:T(256)S(1)} %add_rsqrt_fusion.2), kind=kOutput, calls=%fused_computation.12 | convolution fusion | flops 676397056 | bytes 5395456 | tf_op jit(solution)/shard_map/dot_general | solution.py:302
  122.9 10.7 %convolution_bitcast_fusion = f32[32,8,16,128]{3,1,2,0:T(8,128)S(1)} fusion(bf16[5120,2048]{1,0:T(8,128)(2,1)} %param.14, bf16[256,5120]{1,0:T(8,128)(2,1)} %all-gather.3.cloned.1.call-done, f32[5120]{0:T(1024)S(1)} %copy-done.17, f32[256]{0:T(256)S(1)} %add_rsqrt_fusion.2), kind=kOutput, calls=%fused_computation.10 | convolution fusion | flops 5373952000 | bytes 25711616 | tf_op jit(solution)/shard_map/dot_general | solution.py:291
  133.6 1.8 copy.45
  135.4 0.7 copy-done.14
  136.1 1.4 multiply_reduce_fusion.1
  137.5 0.1 copy.40
  137.6 0.1 multiply_multiply_fusion.1
  137.8 0.2 subtract_convert_fusion.1
  137.9 0.1 maximum_bitcast_fusion
  138.1 0.3 fusion.3
  138.3 0.8 copy.48
  139.1 0.6 multiply_reduce_fusion
  139.7 0.1 copy.38
  139.8 0.1 copy.39
  139.9 0.9 multiply_multiply_fusion
  140.8 0.8 subtract_convert_fusion
  141.6 1.5 pad_maximum_fusion
  143.2 19.9 %all-to-all-done.pages_ref = bf16[32,18,2,16,128]{4,3,2,1,0:T(8,128)(2,1)} async-done(((bf16[32,18,2,16,128]{4,3,2,1,0:T(8,128)(2,1)}), bf16[32,18,2,16,128]{4,3,2,1,0:T(8,128)(2,1)}, u32[]{:S(2)}, u32[]{:S(2)}) %all-to-all-start) | async-done | bytes 4718624 | tf_op jit(solution)/shard_map/all_to_all | solution.py:276
  163.1 6.2 %all-to-all-start.1 = ((bf16[32,6,2,16,128]{4,3,2,1,0:T(8,128)(2,1)}), bf16[32,6,2,16,128]{4,3,2,1,0:T(8,128)(2,1)}, u32[]{:S(2)}, u32[]{:S(2)}) async-start(bf16[32,6,2,16,128]{4,3,2,1,0:T(8,128)(2,1)} %bitcast.10), calls=%async_computation.1 | async-start | bytes 3145728 | tf_op jit(solution)/shard_map/all_to_all | solution.py:276
  169.3 0.3 reduce-window.36
  169.7 0.1 slice.40
  169.8 0.3 reduce-window.24
  170.1 0.1 slice.32
  170.2 0.1 slice_reduce_fusion.1
  170.3 0.1 slice_reduce_fusion.2
  170.4 0.1 add_bitcast_fusion.2
  170.5 0.1 fusion.7
  170.7 0.1 select_reduce_fusion.1.places_ref
  170.8 0.1 add_bitcast_fusion.1
  170.9 0.1 fusion.8
  171.0 0.1 select_reduce_fusion.places_ref
  171.2 0.1 copy_bitcast_fusion.1.k_ref
  171.3 0.3 copy.55
  171.6 14.8 %attend_head.3 = (f32[8,256,256]{2,1,0:T(8,128)S(1)}, f32[8,256,128]{2,1,0:T(8,128)S(1)}) custom-call(s32[2,256]{1,0:T(2,128)S(1)} %select_reduce_fusion.places_ref, s32[1]{0:T(128)} %bitcast.17.length_ref, bf16[256,2048]{1,0:T(8,128)(2,1)S(1)} %bitcast.55, bf16[256,256]{1,0:T(8,128)(2,1)S(1)} %copy_bitcast_fusion.1.k_ref, ...), custom_call_target="tpu_custom_call" | custom-call | flops 4294967296 | bytes 4718592 | tf_op jit(solution)/shard_map/attend_head/pallas_call | solution.py:228
  186.4 1.1 copy-done.4
  187.5 1.4 copy-done.7
  188.9 1.0 copy-done.9
  189.8 1.7 constant_dynamic-slice_fusion
  191.5 1.2 copy-done.5
  192.7 18.6 %attend_head.4.refs_2_ = bf16[256,2048]{1,0:T(8,128)(2,1)} custom-call(s32[2,256]{1,0:T(2,128)S(1)} %get-tuple-element.40.places_ref, s32[1]{0:T(128)} %copy.57.length_ref, bf16[256,2048]{1,0:T(8,128)(2,1)S(1)} %bitcast.56, bf16[256,256]{1,0:T(8,128)(2,1)S(1)} %copy_bitcast_fusion.1.k_ref, bf16[256,256]{1,0:T(8,128)(2,1)S(1)} %convolution_convert_fusion.1.v_ref, ...), custom_call_target="tpu_custom_call" | custom-call | flops 4294967296 | bytes 4718592 | tf_op jit(solution)/shard_map/attend_head/pallas_call | solution.py:228
  211.4 1.2 copy-done.6
  212.6 1.6 copy-done.8
  214.2 1.2 copy-done.10
  215.4 10.7 %attend_head.5 = bf16[256,2048]{1,0:T(8,128)(2,1)} custom-call(s32[2,256]{1,0:T(2,128)S(1)} %select_reduce_fusion.1.places_ref, s32[1]{0:T(128)} %bitcast.5.length_ref, bf16[256,2048]{1,0:T(8,128)(2,1)S(1)} %bitcast.57, bf16[256,256]{1,0:T(8,128)(2,1)S(1)} %copy_bitcast_fusion.1.k_ref, ...), custom_call_target="tpu_custom_call", output_to_operand_aliasing={{}: (8, {})} | custom-call | flops 4294967296 | bytes 1572864 | tf_op jit(solution)/shard_map/attend_head/pallas_call | solution.py:228
  (48 shorter events, 0.4 us)
Async XLA Ops:
  7.2 128.2 %copy-start = (bf16[5120,256]{1,0:T(8,128)(2,1)S(1)}, bf16[5120,256]{1,0:T(8,128)(2,1)}, u32[]{:S(2)}) copy-start(bf16[5120,256]{1,0:T(8,128)(2,1)} %param.15) | copy-start | bytes 7864324
  7.2 110.4 %all-gather.3.cloned.1.call-start = ((), (), s32[]{:S(2)}) async-start(), calls=%async_computation.2 | async-start | bytes 3276800 | tf_op jit(solution)/shard_map/all_gather | solution.py:285
  10.7 2.8 %copy-start.2 = (bf16[96,8,2,16,128]{4,3,2,1,0:T(8,128)(2,1)S(1)}, bf16[96,8,2,16,128]{4,3,2,1,0:T(8,128)(2,1)}, u32[]{:S(2)}) copy-start(bf16[96,8,2,16,128]{4,3,2,1,0:T(8,128)(2,1)} %pool_ref.1) | copy-start | bytes 18874372
  17.5 2.2 copy-start.3
  19.6 7.9 %copy-start.18 = (s32[1,16,1]{1,2,0:T(1,128)S(1)}, s32[1,16,1]{1,2,0:T(1,128)}, u32[]{:S(2)}) copy-start(s32[1,16,1]{1,2,0:T(1,128)} %param.23) | copy-start | bytes 196
  19.6 143.4 %all-to-all-start = ((bf16[32,18,2,16,128]{4,3,2,1,0:T(8,128)(2,1)}), bf16[32,18,2,16,128]{4,3,2,1,0:T(8,128)(2,1)}, u32[]{:S(2)}, u32[]{:S(2)}) async-start(bf16[32,18,2,16,128]{4,3,2,1,0:T(8,128)(2,1)} %bitcast.54), calls=%async_computation | async-start | bytes 9437184 | tf_op jit(solution)/shard_map/all_to_all | solution.py:276
  26.1 94.0 %copy-start.17 = (f32[5120]{0:T(1024)S(1)}, f32[5120]{0:T(1024)}, u32[]{:S(2)}) copy-start(f32[5120]{0:T(1024)} %param.13) | copy-start | bytes 61444
  26.1 163.8 %all-gather.5.cloned.1.call-start = ((), (), s32[]{:S(2)}) async-start(), calls=%async_computation.3 | async-start | bytes 2359296 | tf_op jit(solution)/shard_map/all_gather | solution.py:326
  117.6 2.5 %copy-start.13 = (bf16[256,5120]{1,0:T(8,128)(2,1)S(1)}, bf16[256,5120]{1,0:T(8,128)(2,1)}, u32[]{:S(2)}) copy-start(bf16[256,5120]{1,0:T(8,128)(2,1)} %all-gather.3.cloned.1.call-done) | copy-start | bytes 7864324
  133.6 2.5 %copy-start.14 = (bf16[256,5120]{1,0:T(8,128)(2,1)S(1)}, bf16[256,5120]{1,0:T(8,128)(2,1)}, u32[]{:S(2)}) copy-start(bf16[256,5120]{1,0:T(8,128)(2,1)} %all-gather.3.cloned.1.call-done) | copy-start | bytes 7864324
  136.1 1.5 copy-start.15
  137.5 1.7 copy-start.11
  137.9 2.0 copy-start.16
  143.2 28.1 %copy-start.12 = (bf16[256,16,128]{2,1,0:T(8,128)(2,1)S(1)}, bf16[256,16,128]{2,1,0:T(8,128)(2,1)}, u32[]{:S(2)}) copy-start(bf16[256,16,128]{2,1,0:T(8,128)(2,1)} %pad_maximum_fusion) | copy-start | bytes 3145732
  163.1 48.3 %all-to-all-start.1 = ((bf16[32,6,2,16,128]{4,3,2,1,0:T(8,128)(2,1)}), bf16[32,6,2,16,128]{4,3,2,1,0:T(8,128)(2,1)}, u32[]{:S(2)}, u32[]{:S(2)}) async-start(bf16[32,6,2,16,128]{4,3,2,1,0:T(8,128)(2,1)} %bitcast.10), calls=%async_computation.1 | async-start | bytes 3145728 | tf_op jit(solution)/shard_map/all_to_all | solution.py:276
  186.4 1.1 copy-start.4
  187.5 1.4 copy-start.7
  188.9 1.0 copy-start.9
  191.5 1.2 copy-start.5
  211.4 1.2 copy-start.6
  212.6 1.6 copy-start.8
  214.2 1.2 copy-start.10
  215.4 10.8 %copy-start.1 = (bf16[5120,256]{1,0:T(8,128)(2,1)S(1)}, bf16[5120,256]{1,0:T(8,128)(2,1)}, u32[]{:S(2)}) copy-start(bf16[5120,256]{1,0:T(8,128)(2,1)} %param.15) | copy-start | bytes 7864324
Sparse Core Ops, SparseCore 0:
  9.6 107.9 all-gather.2
  139.2 32.3 all-gather.4
where the time goes:
time: 234 us; the launch traced here: 233 us
  waiting for transfers between devices  109 us (47%)
  Pallas kernels  48.2 us (21%)
  local copies, waits for them, and re-layouts  20.7 us (9%)
  matrix products  15 us (6%)
  between operations  15 us (6%)
  starting transfers between devices  12.7 us (5%)
  other arithmetic  12.2 us (5%)
    all_gather x1, waiting for transfers between devices, shards(): full_rows = lax.all_gather(hidden, 'tensor', axis=1, tiled=True)  88.5 us
    pallas_call x3, Pallas kernels, attend(): pl.pallas_call(functools.partial(attention_kernel, group, scale, base, st...  44.2 us
    all_to_all x2, waiting for transfers between devices, exchange(): lax.all_to_all(pages.reshape((sources,) + pages.shape[2:]), ('dp', 'tenso...  19.9 us
    unnamed x41, local copies, waits for them, and re-layouts  17.2 us
    all_to_all x2, starting transfers between devices, exchange(): lax.all_to_all(pages.reshape((sources,) + pages.shape[2:]), ('dp', 'tenso...  12.7 us
    dot_general x1, matrix products, shards(): jnp.dot(normalized_rows, w_query, preferred_element_type=jnp.float32)  10.7 us
  transfers between devices with their start and end apart: 4, of which 2 were waited for; matrix products, arithmetic and copies ran while one was open for 14% of the time, Pallas kernels for 16%

commit v1 on v0

--- a/solution.py
+++ b/solution.py
@@ -86,7 +86,7 @@
             pl.BlockSpec(memory_space=pltpu.VMEM),
         ],
         out_specs=[block(n) for n in units],
-        compiler_params=pltpu.CompilerParams(vmem_limit_bytes=32 * 2**20),
+        compiler_params=pltpu.CompilerParams(vmem_limit_bytes=60 * 2**20),
         cost_estimate=pl.CostEstimate(flops=0, bytes_accessed=4 * pool.size, transcendentals=0),
         name="gather_pages",
     )(picked.reshape(-1), pool)
@@ -233,7 +233,7 @@
         out_specs=out_specs,
         scratch_shapes=scratch,
         input_output_aliases=aliases,
-        compiler_params=pltpu.CompilerParams(vmem_limit_bytes=44 * 2**20),
+        compiler_params=pltpu.CompilerParams(vmem_limit_bytes=60 * 2**20),
         cost_estimate=pl.CostEstimate(
             flops=4 * rows * part * most * PAGE_TOKENS,
             bytes_accessed=2 * pages.size,
@@ -352,6 +352,8 @@
         attn_out = attend(
             everywhere, prefix_len, *tensors, first_pages, h, key_heads, scale, h * capacity, None, attn_out, True
         )
+    if attn_out is not None:
+        attn_out, first_length = lax.optimization_barrier((attn_out, first_length))
     state = attend(
         first_table, first_length, *tensors, first_pages, last, key_heads, scale, last * capacity, None, None, False
     )

time: 234 us -> 232 us (level)
  local copies, waits for them, and re-layouts: 20.7 us -> 8.67 us
  Pallas kernels: 48.2 us -> 54.7 us
    unnamed x41 -> x27, local copies, waits for them, and re-layouts: 17.2 us -> 4.66 us
    pallas_call x1, Pallas kernels: 3.96 us -> 7.27 us  [gather_pages(): pl.pallas_call(functools.partial(gather_kernel, key_heads, groups, capaci...]
    pallas_call x3, Pallas kernels: 44.2 us -> 47.4 us  [attend(): pl.pallas_call(functools.partial(attention_kernel, group, scale, base, st...]
  transfers between devices with their start and end apart: 4 -> 4, of which waited for: 2 -> 2; matrix products, arithmetic and copies ran while one was open for 14% -> 16% of each run, Pallas kernels for 16% -> 19%
where the time goes in v1:
time: 232 us; the launch traced here: 231 us
  waiting for transfers between devices  110 us (47%)
  Pallas kernels  54.7 us (24%)
  matrix products  15 us (6%)
  between operations  15 us (6%)
  other arithmetic  14.1 us (6%)
  starting transfers between devices  13.1 us (6%)
  local copies, waits for them, and re-layouts  8.67 us (4%)
    all_gather x1, waiting for transfers between devices, shards(): full_rows = lax.all_gather(hidden, 'tensor', axis=1, tiled=True)  90.5 us
    pallas_call x3, Pallas kernels, attend(): pl.pallas_call(functools.partial(attention_kernel, group, scale, base, st...  47.4 us
    all_to_all x2, waiting for transfers between devices, exchange(): lax.all_to_all(pages.reshape((sources,) + pages.shape[2:]), ('dp', 'tenso...  18.9 us
    all_to_all x2, starting transfers between devices, exchange(): lax.all_to_all(pages.reshape((sources,) + pages.shape[2:]), ('dp', 'tenso...  13 us
    dot_general x1, matrix products, shards(): jnp.dot(normalized_rows, w_query, preferred_element_type=jnp.float32)  10.7 us
    pallas_call x1, Pallas kernels, gather_pages(): pl.pallas_call(functools.partial(gather_kernel, key_heads, groups, capaci...  7.27 us
    unnamed x27, local copies, waits for them, and re-layouts  4.66 us
  transfers between devices with their start and end apart: 4, of which 2 were waited for; matrix products, arithmetic and copies ran while one was open for 16% of the time, Pallas kernels for 19%

profile of v1, /device:TPU:7, one launch (start us, length us, event | category | flops | bytes accessed | tf_op | source)
XLA Modules:
  0.0 230.5 jit_solution(17329816836191840426)
XLA Ops:
  7.2 0.0 copy-start
  7.2 0.0 all-gather.3.cloned.1.call-start
  7.2 0.7 all-gather.3.cloned.1.call-update
  7.9 0.7 convert_bitcast_fusion
  8.7 0.6 reduce-window.26
  9.2 0.2 slice_reduce_fusion
  9.5 0.1 add_bitcast_fusion
  9.6 1.0 select_reduce_fusion.2
  10.5 0.1 copy.37
  10.6 0.6 reshape.341.picked_ref
  11.2 7.3 %gather_pages.1 = (bf16[8,4,18,2,16,128]{5,4,3,2,1,0:T(8,128)(2,1)}, bf16[8,4,6,2,16,128]{5,4,3,2,1,0:T(8,128)(2,1)}) custom-call(s32[96]{0:T(128)} %reshape.341.picked_ref, bf16[96,8,2,16,128]{4,3,2,1,0:T(8,128)(2,1)} %pool_ref.1), custom_call_target="tpu_custom_call" | custom-call | bytes 12582912 | tf_op jit(solution)/shard_map/gather_pages/pallas_call | solution.py:80
  18.5 6.4 %all-to-all-start = ((bf16[32,18,2,16,128]{4,3,2,1,0:T(8,128)(2,1)}), bf16[32,18,2,16,128]{4,3,2,1,0:T(8,128)(2,1)}, u32[]{:S(2)}, u32[]{:S(2)}) async-start(bf16[32,18,2,16,128]{4,3,2,1,0:T(8,128)(2,1)} %bitcast.55), calls=%async_computation | async-start | bytes 9437184 | tf_op jit(solution)/shard_map/all_to_all | solution.py:276
  24.9 0.0 copy-start.10
  25.0 0.0 all-gather.5.cloned.1.call-start
  25.7 0.7 constant_dynamic-slice_fusion.1
  26.4 0.2 convert_reduce_fusion.1
  26.6 0.2 convert_reduce_fusion
  26.7 0.7 select_reduce_fusion.3
  27.4 0.5 multiply_cosine_fusion
  27.9 90.5 %all-gather.3.cloned.1.call-done = bf16[256,5120]{1,0:T(8,128)(2,1)} async-done(((bf16[256,1280]{1,0:T(8,128)(2,1)}), bf16[256,5120]{1,0:T(8,128)(2,1)}) %all-gather.3.cloned.1.call-update) | async-done | bytes 2621456 | tf_op jit(solution)/shard_map/all_gather | solution.py:285
  118.4 2.5 %fusion = f32[256]{0:T(256)S(1)} fusion(bf16[256,5120]{1,0:T(8,128)(2,1)} %all-gather.3.cloned.1.call-done), kind=kLoop, calls=%fused_computation.3 | loop fusion | flops 3931904 | bytes 2622464 | tf_op jit(solution)/shard_map/reduce_sum | solution.py:24
  120.9 0.0 copy-done.4
  120.9 2.7 %convolution_convert_fusion.1.v_ref = bf16[256,256]{1,0:T(8,128)(2,1)S(1)} fusion(bf16[5120,256]{1,0:T(8,128)(2,1)} %param.16, bf16[256,5120]{1,0:T(8,128)(2,1)S(1)} %copy-done.4, f32[5120]{0:T(1024)S(1)} %copy-done.10, f32[256]{0:T(256)S(1)} %add_rsqrt_fusion.2), kind=kOutput, calls=%fused_computation.12 | convolution fusion | flops 676397056 | bytes 5395456 | tf_op jit(solution)/shard_map/dot_general | solution.py:302
  123.7 10.7 %convolution_bitcast_fusion = f32[32,8,16,128]{3,1,2,0:T(8,128)S(1)} fusion(bf16[5120,2048]{1,0:T(8,128)(2,1)} %param.14, bf16[256,5120]{1,0:T(8,128)(2,1)} %all-gather.3.cloned.1.call-done, f32[5120]{0:T(1024)S(1)} %copy-done.10, f32[256]{0:T(256)S(1)} %add_rsqrt_fusion.2), kind=kOutput, calls=%fused_computation.10 | convolution fusion | flops 5373952000 | bytes 25711616 | tf_op jit(solution)/shard_map/dot_general | solution.py:291
  134.4 0.0 copy-done.6
  134.4 0.0 copy-start.5
  134.4 1.8 copy.45
  136.2 0.7 copy-done.5
  136.9 1.4 multiply_reduce_fusion.1
  138.3 0.1 copy.40
  138.4 0.1 multiply_multiply_fusion.1
  138.6 0.2 subtract_convert_fusion.1
  138.7 0.0 copy-start.9
  138.7 0.1 maximum_bitcast_fusion
  138.9 0.3 fusion.3
  139.1 0.8 copy.48
  139.9 0.0 all-gather.5.cloned.1.call-update
  139.9 0.6 multiply_reduce_fusion
  140.6 0.1 copy.38
  140.6 0.1 copy.39
  140.7 0.9 multiply_multiply_fusion
  141.6 0.8 subtract_convert_fusion
  142.4 1.5 pad_maximum_fusion
  144.0 18.9 %all-to-all-done.pages_ref = bf16[32,18,2,16,128]{4,3,2,1,0:T(8,128)(2,1)} async-done(((bf16[32,18,2,16,128]{4,3,2,1,0:T(8,128)(2,1)}), bf16[32,18,2,16,128]{4,3,2,1,0:T(8,128)(2,1)}, u32[]{:S(2)}, u32[]{:S(2)}) %all-to-all-start) | async-done | bytes 4718624 | tf_op jit(solution)/shard_map/all_to_all | solution.py:276
  162.9 6.6 %all-to-all-start.1 = ((bf16[32,6,2,16,128]{4,3,2,1,0:T(8,128)(2,1)}), bf16[32,6,2,16,128]{4,3,2,1,0:T(8,128)(2,1)}, u32[]{:S(2)}, u32[]{:S(2)}) async-start(bf16[32,6,2,16,128]{4,3,2,1,0:T(8,128)(2,1)} %bitcast.57), calls=%async_computation.1 | async-start | bytes 3145728 | tf_op jit(solution)/shard_map/all_to_all | solution.py:276
  169.5 0.3 reduce-window.36
  169.8 0.1 slice.40
  169.9 0.3 reduce-window.24
  170.2 0.1 slice.32
  170.3 0.1 slice_reduce_fusion.1
  170.4 0.1 slice_reduce_fusion.2
  170.6 0.1 add_bitcast_fusion.2
  170.7 0.1 fusion.7
  170.8 0.7 select_reduce_fusion.1.places_ref
  171.5 0.1 add_bitcast_fusion.1
  171.6 0.1 fusion.8
  171.8 0.7 select_reduce_fusion.places_ref
  172.5 0.8 copy_bitcast_fusion.1.k_ref
  173.3 1.3 copy.55
  174.6 18.7 %attend_head.3.refs_2_ = bf16[256,2048]{1,0:T(8,128)(2,1)} custom-call(s32[2,256]{1,0:T(2,128)} %copy-done.7, s32[1]{0:T(128)} %copy.57.length_ref, bf16[256,2048]{1,0:T(8,128)(2,1)} %bitcast.61, bf16[256,256]{1,0:T(8,128)(2,1)} %copy_bitcast_fusion.1.k_ref, bf16[256,256]{1,0:T(8,128)(2,1)} %copy-done.6, bf16[32,18,2,16,128]{4,3,2,1,0:T(8,128)(2,1)} %all-to-all-done.pages_ref), custom_call_target="tpu_custom_call" | custom-call | flops 4294967296 | bytes 4718592 | tf_op jit(solution)/shard_map/attend_head/pallas_call | solution.py:228
  193.4 16.8 %attend_head.4 = (f32[8,256,256]{2,1,0:T(8,128)}, f32[8,256,128]{2,1,0:T(8,128)}) custom-call(s32[2,256]{1,0:T(2,128)} %select_reduce_fusion.places_ref, s32[1]{0:T(128)} %bitcast.17.length_ref, bf16[256,2048]{1,0:T(8,128)(2,1)} %bitcast.62, bf16[256,256]{1,0:T(8,128)(2,1)} %copy_bitcast_fusion.1.k_ref, bf16[256,256]{1,0:T(8,128)(2,1)} %copy-done.6, ...), custom_call_target="tpu_custom_call" | custom-call | flops 4294967296 | bytes 4718592 | tf_op jit(solution)/shard_map/attend_head/pallas_call | solution.py:228
  210.2 1.7 constant_dynamic-slice_fusion
  211.8 0.0 all-to-all-done.1.pages_ref
  211.8 11.8 %attend_head.5 = bf16[256,2048]{1,0:T(8,128)(2,1)} custom-call(s32[2,256]{1,0:T(2,128)} %select_reduce_fusion.1.places_ref, s32[1]{0:T(128)} %bitcast.5.length_ref, bf16[256,2048]{1,0:T(8,128)(2,1)} %bitcast.63, bf16[256,256]{1,0:T(8,128)(2,1)} %copy_bitcast_fusion.1.k_ref, bf16[256,256]{1,0:T(8,128)(2,1)} %copy-done.6, ...), custom_call_target="tpu_custom_call", output_to_operand_aliasing={{}: (8, {})} | custom-call | flops 4294967296 | bytes 1572864 | tf_op jit(solution)/shard_map/attend_head/pallas_call | solution.py:228
  (34 shorter events, 0.3 us)
Async XLA Ops:
  7.2 129.0 %copy-start = (bf16[5120,256]{1,0:T(8,128)(2,1)S(1)}, bf16[5120,256]{1,0:T(8,128)(2,1)}, u32[]{:S(2)}) copy-start(bf16[5120,256]{1,0:T(8,128)(2,1)} %param.15) | copy-start | bytes 7864324
  7.2 111.2 %all-gather.3.cloned.1.call-start = ((), (), s32[]{:S(2)}) async-start(), calls=%async_computation.2 | async-start | bytes 3276800 | tf_op jit(solution)/shard_map/all_gather | solution.py:285
  18.5 7.9 %copy-start.11 = (s32[1,16,1]{1,2,0:T(1,128)S(1)}, s32[1,16,1]{1,2,0:T(1,128)}, u32[]{:S(2)}) copy-start(s32[1,16,1]{1,2,0:T(1,128)} %param.23) | copy-start | bytes 196
  18.5 144.4 %all-to-all-start = ((bf16[32,18,2,16,128]{4,3,2,1,0:T(8,128)(2,1)}), bf16[32,18,2,16,128]{4,3,2,1,0:T(8,128)(2,1)}, u32[]{:S(2)}, u32[]{:S(2)}) async-start(bf16[32,18,2,16,128]{4,3,2,1,0:T(8,128)(2,1)} %bitcast.55), calls=%async_computation | async-start | bytes 9437184 | tf_op jit(solution)/shard_map/all_to_all | solution.py:276
  24.9 96.0 %copy-start.10 = (f32[5120]{0:T(1024)S(1)}, f32[5120]{0:T(1024)}, u32[]{:S(2)}) copy-start(f32[5120]{0:T(1024)} %param.13) | copy-start | bytes 61444
  25.0 185.2 %all-gather.5.cloned.1.call-start = ((), (), s32[]{:S(2)}) async-start(), calls=%async_computation.3 | async-start | bytes 2359296 | tf_op jit(solution)/shard_map/all_gather | solution.py:326
  118.4 2.5 %copy-start.4 = (bf16[256,5120]{1,0:T(8,128)(2,1)S(1)}, bf16[256,5120]{1,0:T(8,128)(2,1)}, u32[]{:S(2)}) copy-start(bf16[256,5120]{1,0:T(8,128)(2,1)} %all-gather.3.cloned.1.call-done) | copy-start | bytes 7864324
  123.6 10.8 %copy-start.6 = (bf16[256,256]{1,0:T(8,128)(2,1)}, bf16[256,256]{1,0:T(8,128)(2,1)S(1)}, u32[]{:S(2)}) copy-start(bf16[256,256]{1,0:T(8,128)(2,1)S(1)} %convolution_convert_fusion.1.v_ref) | copy-start | bytes 393220
  134.4 2.5 %copy-start.5 = (bf16[256,5120]{1,0:T(8,128)(2,1)S(1)}, bf16[256,5120]{1,0:T(8,128)(2,1)}, u32[]{:S(2)}) copy-start(bf16[256,5120]{1,0:T(8,128)(2,1)} %all-gather.3.cloned.1.call-done) | copy-start | bytes 7864324
  136.9 1.5 copy-start.8
  138.3 1.7 copy-start.2
  138.7 2.0 copy-start.9
  144.0 29.3 %copy-start.3 = (bf16[256,16,128]{2,1,0:T(8,128)(2,1)S(1)}, bf16[256,16,128]{2,1,0:T(8,128)(2,1)}, u32[]{:S(2)}) copy-start(bf16[256,16,128]{2,1,0:T(8,128)(2,1)} %pad_maximum_fusion) | copy-start | bytes 3145732
  162.9 48.9 %all-to-all-start.1 = ((bf16[32,6,2,16,128]{4,3,2,1,0:T(8,128)(2,1)}), bf16[32,6,2,16,128]{4,3,2,1,0:T(8,128)(2,1)}, u32[]{:S(2)}, u32[]{:S(2)}) async-start(bf16[32,6,2,16,128]{4,3,2,1,0:T(8,128)(2,1)} %bitcast.57), calls=%async_computation.1 | async-start | bytes 3145728 | tf_op jit(solution)/shard_map/all_to_all | solution.py:276
  170.6 4.0 %copy-start.7 = (s32[2,256]{1,0:T(2,128)}, s32[2,256]{1,0:T(2,128)S(1)}, u32[]{:S(2)}) copy-start(s32[2,256]{1,0:T(2,128)S(1)} %get-tuple-element.44.places_ref) | copy-start | bytes 6148
  211.8 11.8 %copy-start.1 = (bf16[5120,256]{1,0:T(8,128)(2,1)S(1)}, bf16[5120,256]{1,0:T(8,128)(2,1)}, u32[]{:S(2)}) copy-start(bf16[5120,256]{1,0:T(8,128)(2,1)} %param.15) | copy-start | bytes 7864324
Sparse Core Ops, SparseCore 0:
  9.6 108.7 all-gather.2
  140.0 32.4 all-gather.4

commit v2 on v1

--- a/solution.py
+++ b/solution.py
@@ -268,7 +268,7 @@
     own_row = lax.dynamic_index_in_dim(page_owner, request, 0, keepdims=False)
     my_device = request * tensor_ways + lax.axis_index("tensor")
     picked, unused = collect(page_owner == my_device, page_slot, capacity)
-    early = max(1, capacity // 2)
+    early = max(1, capacity // 3)
     outgoing = gather_pages(picked, kv_pool, key_heads, early)
     sources = data_ways * tensor_ways
 

time: 232 us -> 228 us (0.983)
  Pallas kernels: 54.7 us -> 47.4 us
  matrix products: 15 us -> 12.5 us
    pallas_call x3, Pallas kernels: 47.4 us -> 40.2 us  [attend(): pl.pallas_call(functools.partial(attention_kernel, group, scale, base, st...]
    all_gather x1, waiting for transfers between devices: 0.01 us -> 4.06 us  [shards(): every = lax.all_gather(outgoing_pages, 'dp', axis=0)]
    all_to_all x2, waiting for transfers between devices: 18.9 us -> 15.5 us  [exchange(): lax.all_to_all(pages.reshape((sources,) + pages.shape[2:]), ('dp', 'tenso...]
    unnamed x27 -> x29, local copies, waits for them, and re-layouts: 4.66 us -> 4.42 us
  transfers between devices with their start and end apart: 4 -> 4, of which waited for: 2 -> 4; matrix products, arithmetic and copies ran while one was open for 16% -> 16% of each run, Pallas kernels for 19% -> 16%
where the time goes in v2:
time: 228 us; the launch traced here: 224 us
  waiting for transfers between devices  112 us (49%)
  Pallas kernels  47.4 us (21%)
  other arithmetic  15.8 us (7%)
  between operations  15 us (7%)
  starting transfers between devices  12.7 us (6%)
  matrix products  12.5 us (5%)
  local copies, waits for them, and re-layouts  8.43 us (4%)
    all_gather x1, waiting for transfers between devices, shards(): full_rows = lax.all_gather(hidden, 'tensor', axis=1, tiled=True)  92.3 us
    pallas_call x3, Pallas kernels, attend(): pl.pallas_call(functools.partial(attention_kernel, group, scale, base, st...  40.2 us
    all_to_all x2, waiting for transfers between devices, exchange(): lax.all_to_all(pages.reshape((sources,) + pages.shape[2:]), ('dp', 'tenso...  15.5 us
    all_to_all x2, starting transfers between devices, exchange(): lax.all_to_all(pages.reshape((sources,) + pages.shape[2:]), ('dp', 'tenso...  12.7 us
    dot_general x1, matrix products, shards(): jnp.dot(normalized_rows, w_query, preferred_element_type=jnp.float32)  9.9 us
    pallas_call x1, Pallas kernels, gather_pages(): pl.pallas_call(functools.partial(gather_kernel, key_heads, groups, capaci...  7.21 us
    reduce_sum x2, other arithmetic, rms_rows(): mean_square = jnp.mean(values * values, axis=-1, keepdims=True)  4.82 us
  transfers between devices with their start and end apart: 4, of which 4 were waited for; matrix products, arithmetic and copies ran while one was open for 16% of the time, Pallas kernels for 16%

profile of v2, /device:TPU:7, one launch (start us, length us, event | category | flops | bytes accessed | tf_op | source)
XLA Modules:
  0.0 224.4 jit_solution(11400617859330153833)
XLA Ops:
  7.2 0.0 copy-start
  7.2 0.0 all-gather.3.cloned.1.call-start
  7.2 0.7 all-gather.3.cloned.1.call-update
  7.9 0.7 convert_bitcast_fusion
  8.7 0.6 reduce-window.26
  9.2 0.2 slice_reduce_fusion
  9.5 0.1 add_bitcast_fusion
  9.6 1.0 select_reduce_fusion.2
  10.5 0.1 copy.37
  10.6 0.6 reshape.341.picked_ref
  11.2 7.2 %gather_pages.1 = (bf16[8,4,16,2,16,128]{5,4,3,2,1,0:T(8,128)(2,1)}, bf16[8,4,8,2,16,128]{5,4,3,2,1,0:T(8,128)(2,1)}) custom-call(s32[96]{0:T(128)} %reshape.341.picked_ref, bf16[96,8,2,16,128]{4,3,2,1,0:T(8,128)(2,1)} %pool_ref.1), custom_call_target="tpu_custom_call" | custom-call | bytes 12582912 | tf_op jit(solution)/shard_map/gather_pages/pallas_call | solution.py:80
  18.4 6.4 %all-to-all-start = ((bf16[32,16,2,16,128]{4,3,2,1,0:T(8,128)(2,1)}), bf16[32,16,2,16,128]{4,3,2,1,0:T(8,128)(2,1)}, u32[]{:S(2)}, u32[]{:S(2)}) async-start(bf16[32,16,2,16,128]{4,3,2,1,0:T(8,128)(2,1)} %bitcast.56), calls=%async_computation | async-start | bytes 8388608 | tf_op jit(solution)/shard_map/all_to_all | solution.py:276
  25.6 0.7 constant_dynamic-slice_fusion.1
  26.3 0.2 convert_reduce_fusion.1
  26.5 0.2 convert_reduce_fusion
  26.7 0.7 select_reduce_fusion.3
  27.4 0.5 multiply_cosine_fusion
  27.9 92.3 %all-gather.3.cloned.1.call-done = bf16[256,5120]{1,0:T(8,128)(2,1)} async-done(((bf16[256,1280]{1,0:T(8,128)(2,1)}), bf16[256,5120]{1,0:T(8,128)(2,1)}) %all-gather.3.cloned.1.call-update) | async-done | bytes 2621456 | tf_op jit(solution)/shard_map/all_gather | solution.py:285
  120.2 2.5 %fusion = f32[256]{0:T(256)S(1)} fusion(bf16[256,5120]{1,0:T(8,128)(2,1)} %all-gather.3.cloned.1.call-done), kind=kLoop, calls=%fused_computation.3 | loop fusion | flops 3931904 | bytes 2622464 | tf_op jit(solution)/shard_map/reduce_sum | solution.py:24
  122.7 0.0 copy-done.4
  122.7 9.9 %convolution_bitcast_fusion = f32[32,8,16,128]{3,1,2,0:T(8,128)S(1)} fusion(bf16[5120,2048]{1,0:T(8,128)(2,1)} %param.14, bf16[256,5120]{1,0:T(8,128)(2,1)S(1)} %copy-done.4, f32[5120]{0:T(1024)S(1)} %copy-done.11, f32[256]{0:T(256)S(1)} %add_rsqrt_fusion.2), kind=kOutput, calls=%fused_computation.10 | convolution fusion | flops 5373952000 | bytes 25711616 | tf_op jit(solution)/shard_map/dot_general | solution.py:291
  132.6 1.7 copy.45
  134.3 1.4 multiply_reduce_fusion.1
  135.7 0.0 copy-start.8
  135.7 0.1 copy.40
  135.8 2.3 %multiply_reduce_fusion = f32[256,16]{1,0:T(8,128)S(1)} fusion(f32[256,16,128]{2,1,0:T(8,128)} %bitcast.54), kind=kLoop, calls=%fused_computation.9 | loop fusion | flops 1044480 | bytes 2113536 | tf_op jit(solution)/shard_map/reduce_sum | solution.py:24
  138.1 0.1 copy.38
  138.2 0.1 copy.39
  138.3 0.9 multiply_multiply_fusion
  139.2 0.0 copy-start.10
  139.2 0.8 subtract_convert_fusion
  140.0 1.5 pad_maximum_fusion
  141.6 0.1 multiply_multiply_fusion.1
  141.7 0.6 copy-done.5
  142.4 0.9 convolution_convert_fusion.1.v_ref
  143.3 8.7 %all-to-all-done.pages_ref = bf16[32,16,2,16,128]{4,3,2,1,0:T(8,128)(2,1)} async-done(((bf16[32,16,2,16,128]{4,3,2,1,0:T(8,128)(2,1)}), bf16[32,16,2,16,128]{4,3,2,1,0:T(8,128)(2,1)}, u32[]{:S(2)}, u32[]{:S(2)}) %all-to-all-start) | async-done | bytes 4194336 | tf_op jit(solution)/shard_map/all_to_all | solution.py:276
  152.0 6.2 %all-to-all-start.1 = ((bf16[32,8,2,16,128]{4,3,2,1,0:T(8,128)(2,1)}), bf16[32,8,2,16,128]{4,3,2,1,0:T(8,128)(2,1)}, u32[]{:S(2)}, u32[]{:S(2)}) async-start(bf16[32,8,2,16,128]{4,3,2,1,0:T(8,128)(2,1)} %bitcast.57), calls=%async_computation.1 | async-start | bytes 4194304 | tf_op jit(solution)/shard_map/all_to_all | solution.py:276
  158.2 0.0 copy-start.3
  158.2 0.0 all-gather.5.cloned.1.call-start
  158.3 0.2 subtract_convert_fusion.1
  158.5 0.1 maximum_bitcast_fusion
  158.7 0.3 fusion.3
  158.9 0.8 copy.48
  159.7 0.0 all-gather.5.cloned.1.call-update
  159.7 0.3 reduce-window.36
  160.0 0.1 slice.40
  160.1 0.3 reduce-window.24
  160.5 0.1 slice.32
  160.6 0.1 slice_reduce_fusion.1
  160.7 0.1 slice_reduce_fusion.2
  160.8 0.1 add_bitcast_fusion.2
  160.9 0.1 fusion.7
  161.0 0.7 select_reduce_fusion.1.places_ref
  161.8 0.1 add_bitcast_fusion.1
  161.8 0.1 fusion.8
  162.0 0.7 select_reduce_fusion.places_ref
  162.7 0.8 copy_bitcast_fusion.1.k_ref
  163.5 1.3 copy.55
  164.8 15.1 %attend_head.3.refs_2_ = bf16[256,2048]{1,0:T(8,128)(2,1)} custom-call(s32[2,256]{1,0:T(2,128)} %copy-done.7, s32[1]{0:T(128)} %copy.57.length_ref, bf16[256,2048]{1,0:T(8,128)(2,1)} %bitcast.61, bf16[256,256]{1,0:T(8,128)(2,1)} %copy_bitcast_fusion.1.k_ref, bf16[256,256]{1,0:T(8,128)(2,1)} %copy-done.6, bf16[32,16,2,16,128]{4,3,2,1,0:T(8,128)(2,1)} %all-to-all-done.pages_ref), custom_call_target="tpu_custom_call" | custom-call | flops 4294967296 | bytes 4194304 | tf_op jit(solution)/shard_map/attend_head/pallas_call | solution.py:228
  179.8 13.1 %attend_head.4 = (f32[8,256,256]{2,1,0:T(8,128)}, f32[8,256,128]{2,1,0:T(8,128)}) custom-call(s32[2,256]{1,0:T(2,128)} %select_reduce_fusion.places_ref, s32[1]{0:T(128)} %bitcast.17.length_ref, bf16[256,2048]{1,0:T(8,128)(2,1)} %bitcast.62, bf16[256,256]{1,0:T(8,128)(2,1)} %copy_bitcast_fusion.1.k_ref, bf16[256,256]{1,0:T(8,128)(2,1)} %copy-done.6, ...), custom_call_target="tpu_custom_call" | custom-call | flops 4294967296 | bytes 4194304 | tf_op jit(solution)/shard_map/attend_head/pallas_call | solution.py:228
  193.0 4.1 %all-gather.5.cloned.1.call-done = bf16[8,8,2,2,2,16,128]{6,5,4,3,2,1,0:T(8,128)(2,1)} async-done(((bf16[1,8,2,2,2,16,128]{6,5,4,3,2,1,0:T(8,128)(2,1)}), bf16[8,8,2,2,2,16,128]{6,5,4,3,2,1,0:T(8,128)(2,1)}) %all-gather.5.cloned.1.call-update) | async-done | bytes 2097168 | tf_op jit(solution)/shard_map/all_gather | solution.py:326
  197.0 1.7 constant_dynamic-slice_fusion
  198.7 6.8 %all-to-all-done.1.pages_ref = bf16[32,8,2,16,128]{4,3,2,1,0:T(8,128)(2,1)} async-done(((bf16[32,8,2,16,128]{4,3,2,1,0:T(8,128)(2,1)}), bf16[32,8,2,16,128]{4,3,2,1,0:T(8,128)(2,1)}, u32[]{:S(2)}, u32[]{:S(2)}) %all-to-all-start.1) | async-done | bytes 2097184 | tf_op jit(solution)/shard_map/all_to_all | solution.py:276
  205.5 12.0 %attend_head.5 = bf16[256,2048]{1,0:T(8,128)(2,1)} custom-call(s32[2,256]{1,0:T(2,128)} %select_reduce_fusion.1.places_ref, s32[1]{0:T(128)} %bitcast.5.length_ref, bf16[256,2048]{1,0:T(8,128)(2,1)} %bitcast.63, bf16[256,256]{1,0:T(8,128)(2,1)} %copy_bitcast_fusion.1.k_ref, bf16[256,256]{1,0:T(8,128)(2,1)} %copy-done.6, ...), custom_call_target="tpu_custom_call", output_to_operand_aliasing={{}: (8, {})} | custom-call | flops 4294967296 | bytes 2097152 | tf_op jit(solution)/shard_map/attend_head/pallas_call | solution.py:228
  (36 shorter events, 0.3 us)
Async XLA Ops:
  7.2 127.1 %copy-start = (bf16[5120,256]{1,0:T(8,128)(2,1)S(1)}, bf16[5120,256]{1,0:T(8,128)(2,1)}, u32[]{:S(2)}) copy-start(bf16[5120,256]{1,0:T(8,128)(2,1)} %param.15) | copy-start | bytes 7864324
  7.2 113.0 %all-gather.3.cloned.1.call-start = ((), (), s32[]{:S(2)}) async-start(), calls=%async_computation.2 | async-start | bytes 3276800 | tf_op jit(solution)/shard_map/all_gather | solution.py:285
  18.4 7.8 %copy-start.12 = (s32[1,16,1]{1,2,0:T(1,128)S(1)}, s32[1,16,1]{1,2,0:T(1,128)}, u32[]{:S(2)}) copy-start(s32[1,16,1]{1,2,0:T(1,128)} %param.23) | copy-start | bytes 196
  18.4 133.6 %all-to-all-start = ((bf16[32,16,2,16,128]{4,3,2,1,0:T(8,128)(2,1)}), bf16[32,16,2,16,128]{4,3,2,1,0:T(8,128)(2,1)}, u32[]{:S(2)}, u32[]{:S(2)}) async-start(bf16[32,16,2,16,128]{4,3,2,1,0:T(8,128)(2,1)} %bitcast.56), calls=%async_computation | async-start | bytes 8388608 | tf_op jit(solution)/shard_map/all_to_all | solution.py:276
  24.9 97.8 %copy-start.11 = (f32[5120]{0:T(1024)S(1)}, f32[5120]{0:T(1024)}, u32[]{:S(2)}) copy-start(f32[5120]{0:T(1024)} %param.13) | copy-start | bytes 61444
  120.2 2.5 %copy-start.4 = (bf16[256,5120]{1,0:T(8,128)(2,1)S(1)}, bf16[256,5120]{1,0:T(8,128)(2,1)}, u32[]{:S(2)}) copy-start(bf16[256,5120]{1,0:T(8,128)(2,1)} %all-gather.3.cloned.1.call-done) | copy-start | bytes 7864324
  135.6 2.7 %copy-start.2 = (f32[32,8,16,128]{3,2,1,0:T(8,128)S(1)}, f32[32,8,16,128]{3,2,1,0:T(8,128)}, u32[]{:S(2)}) copy-start(f32[32,8,16,128]{3,2,1,0:T(8,128)} %copy.45) | copy-start | bytes 6291460
  135.7 2.7 %copy-start.8 = (f32[128]{0:T(128)S(1)}, f32[128]{0:T(128)}, u32[]{:S(2)}) copy-start(f32[128]{0:T(128)} %param.17) | copy-start | bytes 1540
  139.2 2.5 %copy-start.10 = (bf16[5120,256]{1,0:T(8,128)(2,1)S(1)}, bf16[5120,256]{1,0:T(8,128)(2,1)}, u32[]{:S(2)}) copy-start(bf16[5120,256]{1,0:T(8,128)(2,1)} %param.16) | copy-start | bytes 7864324
  140.0 1.6 copy-start.9
  140.0 2.4 %copy-start.5 = (bf16[256,5120]{1,0:T(8,128)(2,1)S(1)}, bf16[256,5120]{1,0:T(8,128)(2,1)}, u32[]{:S(2)}) copy-start(bf16[256,5120]{1,0:T(8,128)(2,1)} %all-gather.3.cloned.1.call-done) | copy-start | bytes 7864324
  143.3 15.2 %copy-start.6 = (bf16[256,256]{1,0:T(8,128)(2,1)}, bf16[256,256]{1,0:T(8,128)(2,1)S(1)}, u32[]{:S(2)}) copy-start(bf16[256,256]{1,0:T(8,128)(2,1)S(1)} %convolution_convert_fusion.1.v_ref) | copy-start | bytes 393220
  152.0 53.5 %all-to-all-start.1 = ((bf16[32,8,2,16,128]{4,3,2,1,0:T(8,128)(2,1)}), bf16[32,8,2,16,128]{4,3,2,1,0:T(8,128)(2,1)}, u32[]{:S(2)}, u32[]{:S(2)}) async-start(bf16[32,8,2,16,128]{4,3,2,1,0:T(8,128)(2,1)} %bitcast.57), calls=%async_computation.1 | async-start | bytes 4194304 | tf_op jit(solution)/shard_map/all_to_all | solution.py:276
  158.2 5.3 %copy-start.3 = (bf16[256,16,128]{2,1,0:T(8,128)(2,1)S(1)}, bf16[256,16,128]{2,1,0:T(8,128)(2,1)}, u32[]{:S(2)}) copy-start(bf16[256,16,128]{2,1,0:T(8,128)(2,1)} %pad_maximum_fusion) | copy-start | bytes 3145732
  158.2 38.8 %all-gather.5.cloned.1.call-start = ((), (), s32[]{:S(2)}) async-start(), calls=%async_computation.3 | async-start | bytes 2359296 | tf_op jit(solution)/shard_map/all_gather | solution.py:326
  160.8 3.9 %copy-start.7 = (s32[2,256]{1,0:T(2,128)}, s32[2,256]{1,0:T(2,128)S(1)}, u32[]{:S(2)}) copy-start(s32[2,256]{1,0:T(2,128)S(1)} %get-tuple-element.44.places_ref) | copy-start | bytes 6148
  205.5 12.0 %copy-start.1 = (bf16[5120,256]{1,0:T(8,128)(2,1)S(1)}, bf16[5120,256]{1,0:T(8,128)(2,1)}, u32[]{:S(2)}) copy-start(bf16[5120,256]{1,0:T(8,128)(2,1)} %param.15) | copy-start | bytes 7864324
Sparse Core Ops, SparseCore 0:
  9.6 110.5 all-gather.2
  161.5 35.4 all-gather.4
